TPU v7x, 32 devices: a whole 2x2x4 slice. The times are simulated.
32 devices in a mesh: groups: 2 (over y), expert: 4 (over z), helper: 2 (over x), sub: 2 (over core).
Axes of the slice: x: 2, y: 2, z: 4, core: 2. Of those that a mesh axis runs over, the one named last changes fastest.
Arguments:
- tokens: bfloat16 [1024, 7168], P(('groups', 'expert'), ('helper', 'sub')), parts along dimension 0, may hold values from -6 to 6
- routes: int32 [1024, 8], P(('groups', 'expert')), parts along dimension 0, may hold values from 0 to 15, all different within a row; in each aligned block of 128 rows (0 to 127, 128 to 255, ...) at most 72 rows name the same one
- router_weight: bfloat16 [7168, 16], P(('helper', 'sub')), may hold values from -0.0625 to 0.0625
- gate_weight: bfloat16 [16, 7168, 2048], P('expert', None, ('helper', 'sub')), may hold values from -0.0625 to 0.0625
- up_weight: bfloat16 [16, 7168, 2048], P('expert', None, ('helper', 'sub')), may hold values from -0.0625 to 0.0625
- down_weight: bfloat16 [16, 2048, 7168], P('expert', None, ('helper', 'sub')), may hold values from -0.125 to 0.125
Outputs:
- mixed: bfloat16 [1024, 7168], P(('groups', 'expert'), ('helper', 'sub')), parts along dimension 0
- zloss: float32 [1024], P(('groups', 'expert')), parts along dimension 0
There are 2 independent parts, one for each index of `groups`. A program takes and returns all parts, laid end to end along the dimension named above; an argument that names none is the same for every part. Nothing has to cross between parts.
Inputs may be any that keep to these rules, and one draw needn't show every extreme that they name: `routes`: in each aligned block of 128 rows (the rows of one index of the expert axis) a row names 8 different experts, no expert is named by more than 72 rows, a bound that some block reaches.
All inputs are finite; a program needn't handle non-finite values.
Results may differ from a plain program's by a relative error of at most 0.0064.
Values may be sent and summed in bfloat16 or wider, within the bound.
A program may use at most 256 MiB of HBM per device.

v0:
```python
import jax
import jax.numpy as jnp
from jax import lax
from jax.sharding import PartitionSpec as P

CAP = 72


def slot_of(block_routes, count, capacity):
    flat = block_routes.reshape(-1)
    table = (flat[:, None] == jnp.arange(count, dtype=jnp.int32)[None, :]).astype(jnp.int32)
    before = jnp.cumsum(table, axis=0) - table
    place = jnp.sum(before * table, axis=1)
    return flat * capacity + place


def source_of(slots, rows, top, count, capacity):
    owner = jnp.arange(rows * top, dtype=jnp.int32) // top
    return jnp.full((count * capacity,), rows, jnp.int32).at[slots].set(owner)


def body(tokens, routes, router_weight, gate_weight, up_weight, down_weight):
    tok_rows = tokens.shape[0]
    top_count = routes.shape[1]
    expert_count = router_weight.shape[1]
    homes = lax.axis_size("expert")
    local_experts = gate_weight.shape[0]
    capacity = CAP
    partial_logits = jnp.dot(tokens, router_weight, preferred_element_type=jnp.float32)
    logits = lax.psum(partial_logits, ("helper", "sub"))
    zloss = jnp.square(jnp.log(jnp.sum(jnp.exp(logits), axis=1)))
    picks = routes[:, :, None] == jnp.arange(expert_count, dtype=jnp.int32)[None, None, :]
    chosen = jnp.sum(jnp.where(picks, logits[:, None, :], 0.0), axis=2)
    affinity = jax.nn.sigmoid(chosen)
    gates = (2.5 * affinity / jnp.sum(affinity, axis=1, keepdims=True)).astype(jnp.bfloat16)
    slots = slot_of(routes, expert_count, capacity)
    sources = source_of(slots, tok_rows, top_count, expert_count, capacity)
    features = lax.all_gather(tokens, ("helper", "sub"), axis=1, tiled=True)
    padded = jnp.concatenate([features, jnp.zeros((1, features.shape[1]), jnp.bfloat16)], axis=0)
    buffer = padded[sources].reshape(homes, local_experts, capacity, features.shape[1])
    received = lax.all_to_all(buffer, "expert", split_axis=0, concat_axis=0, tiled=True)
    gate = jnp.einsum("nlcd,ldf->nlcf", received, gate_weight, preferred_element_type=jnp.float32)
    up = jnp.einsum("nlcd,ldf->nlcf", received, up_weight, preferred_element_type=jnp.float32)
    hidden = (jax.nn.silu(gate) * up).astype(jnp.bfloat16)
    answer = jnp.einsum(
        "nlcf,lfd->nlcd",
        lax.all_gather(hidden, ("helper", "sub"), axis=3, tiled=True),
        down_weight,
        preferred_element_type=jnp.float32,
    )
    returned = lax.all_to_all(
        answer.astype(jnp.bfloat16), "expert", split_axis=0, concat_axis=0, tiled=True
    )
    flat_answers = returned.reshape(expert_count * capacity, returned.shape[3])
    picked = flat_answers[slots].reshape(tok_rows, top_count, returned.shape[3])
    mixed = jnp.einsum("tk,tkd->td", gates, picked, preferred_element_type=jnp.float32)
    return (mixed.astype(jnp.bfloat16), zloss)


def solution(mesh):
    placed = (
        P(("groups", "expert"), ("helper", "sub")),
        P(("groups", "expert"), None),
        P(("helper", "sub"), None),
        P("expert", None, ("helper", "sub")),
        P("expert", None, ("helper", "sub")),
        P("expert", None, ("helper", "sub")),
    )
    return jax.shard_map(
        body,
        mesh=mesh,
        in_specs=placed,
        out_specs=(P(("groups", "expert"), ("helper", "sub")), P(("groups", "expert"))),
        check_vma=False,
    )
```

profile of v0, /device:TPU:8, one launch (start us, length us, event | category | flops | bytes accessed | tf_op | source)
XLA Modules:
  0.0 634.7 jit_solution(1748041007178679807)
XLA Ops:
  7.2 0.0 copy-start
  7.2 0.0 all-gather.3.cloned.1.call-start
  7.2 0.7 all-gather.3.cloned.1.call-update
  7.9 0.0 all-gather.5.cloned.1.call-start
  8.0 0.8 copy.32
  8.7 0.1 eq.45
  8.8 0.1 eq.41
  8.9 4.5 reduce-window.6
  13.5 0.1 slice.12
  13.5 0.1 copy.34
  13.7 0.1 copy.35
  13.8 0.7 broadcast_multiply_fusion
  14.5 0.1 copy.31
  14.6 0.1 mul.36
  14.7 0.1 broadcast_add_fusion
  14.8 4.3 scatter_custom_fusion
  19.2 12.7 %all-gather.3.cloned.1.call-done = bf16[128,7168]{1,0:T(8,128)(2,1)} async-done(((bf16[128,1792]{1,0:T(8,128)(2,1)}), bf16[128,7168]{1,0:T(8,128)(2,1)}) %all-gather.3.cloned.1.call-update) | async-done | bytes 1835024 | tf_op jit(solution)/shard_map/all_gather | solution.py:38
  31.9 1.7 concatenate.3
  33.6 13.5 %gather_fusion = bf16[1152,7168]{1,0:T(8,128)(2,1)} fusion(bf16[129,7168]{1,0:T(8,128)(2,1)S(1)} %concatenate.3, s32[2048]{0:T(1024)S(1)} %pad_clamp_fusion), kind=kCustom, calls=%fused_computation | custom fusion | bytes 33034752 | tf_op jit(solution)/shard_map/gather | solution.py:40
  47.1 367.5 %all_to_all.10 = bf16[4,4,72,7168]{3,2,1,0:T(8,128)(2,1)} all-to-all(bf16[4,4,72,7168]{3,2,1,0:T(8,128)(2,1)} %bitcast.72), channel_id=1, replica_groups=mesh['groups'=2,'expert'=4,'helper'=2,'sub'=2] {'expert'}, dimensions={0} | all-to-all | bytes 33030144 | tf_op jit(solution)/shard_map/all_to_all | solution.py:41
  414.6 20.0 %fusion.2 = f32[4,4,72,512]{3,2,1,0:T(8,128)} fusion(bf16[4,7168,512]{2,1,0:T(8,128)(2,1)} %param.10, bf16[4,4,72,7168]{3,2,1,0:T(8,128)(2,1)} %all_to_all.10), kind=kOutput, calls=%fused_computation.5 | convolution fusion | flops 8455716864 | bytes 48234496 | tf_op jit(solution)/shard_map/nlcd,ldf->nlcf/dot_general | solution.py:43
  434.6 28.0 %fusion.12 = bf16[4,4,72,512]{3,2,0,1:T(8,128)(2,1)} fusion(f32[4,4,72,512]{3,2,1,0:T(8,128)} %fusion.2, bf16[4,7168,512]{2,1,0:T(8,128)(2,1)} %param.9, bf16[4,4,72,7168]{3,2,1,0:T(8,128)(2,1)} %all_to_all.10), kind=kOutput, calls=%fused_computation.15 | convolution fusion | flops 8459255808 | bytes 49414144 | tf_op jit(solution)/shard_map/nlcd,ldf->nlcf/dot_general | solution.py:42
  462.6 0.0 all-gather.5.cloned.1.call-update
  462.6 37.0 %all-gather.5.cloned.1.call-done = bf16[4,4,72,2048]{3,2,0,1:T(8,128)(2,1)} async-done(((bf16[4,4,72,512]{3,2,0,1:T(8,128)(2,1)}), bf16[4,4,72,2048]{3,2,0,1:T(8,128)(2,1)}) %all-gather.5.cloned.1.call-update) | async-done | bytes 4718608 | tf_op jit(solution)/shard_map/all_gather | solution.py:47
  499.6 16.8 %convert_bitcast_fusion = bf16[4,4,72,1792]{3,2,0,1:T(8,128)(2,1)S(1)} fusion(bf16[4,4,72,2048]{3,2,0,1:T(8,128)(2,1)} %all-gather.5.cloned.1.call-done, bf16[4,2048,1792]{2,1,0:T(8,128)(2,1)} %param.11), kind=kOutput, calls=%fused_computation.11 | convolution fusion | flops 8457781248 | bytes 38207488 | tf_op jit(solution)/shard_map/nlcf,lfd->nlcd/dot_general | solution.py:45
  516.5 2.2 copy.38
  518.7 0.0 copy-start.1
  518.7 0.0 copy-start.2
  518.7 5.5 all-to-all-start.1
  524.2 0.0 copy-done
  524.2 0.0 copy-done.1
  524.2 0.2 fusion.31
  524.4 6.4 %psum.7 = f32[128,16]{0,1:T(8,128)S(1)} all-reduce(f32[128,16]{0,1:T(8,128)S(1)} %fusion.31), channel_id=1, replica_groups=mesh['groups'=2,'expert'=4,'helper'=2,'sub'=2] {'helper','sub'}, use_global_device_ids=true, to_apply=%region_0.0 | all-reduce | flops 2048 | bytes 16384 | tf_op jit(solution)/shard_map/psum | solution.py:30
  530.8 0.0 copy-done.2
  530.9 0.1 copy.42
  531.0 0.5 log_multiply_fusion
  531.6 81.8 %all-to-all-done.1 = bf16[4,4,72,1792]{3,2,1,0:T(8,128)(2,1)} async-done(((bf16[4,4,72,1792]{3,2,1,0:T(8,128)(2,1)}), bf16[4,4,72,1792]{3,2,1,0:T(8,128)(2,1)}, u32[]{:S(2)}, u32[]{:S(2)}) %all-to-all-start.1) | async-done | bytes 4128800 | tf_op jit(solution)/shard_map/all_to_all | solution.py:51
  613.3 10.6 %gather_fusion.1 = bf16[1024,1792]{1,0:T(8,128)(2,1)} fusion(bf16[1152,1792]{1,0:T(8,128)(2,1)} %bitcast.15, s32[1024]{0:T(1024)S(1)} %broadcast_clamp_fusion), kind=kCustom, calls=%fused_computation.1 | custom fusion | bytes 7344128 | tf_op jit(solution)/shard_map/gather | solution.py:55
  623.9 3.1 fusion.10
  627.1 0.8 copy.53
  (13 shorter events, 0.2 us)
Async XLA Ops:
  7.2 517.0 %copy-start = (bf16[1792,16]{0,1:T(8,128)(2,1)S(1)}, bf16[1792,16]{0,1:T(8,128)(2,1)}, u32[]{:S(2)}) copy-start(bf16[1792,16]{0,1:T(8,128)(2,1)} %param.8) | copy-start | bytes 172036
  7.2 24.7 %all-gather.3.cloned.1.call-start = ((), (), s32[]{:S(2)}) async-start(), calls=%async_computation.2 | async-start | bytes 2293760 | tf_op jit(solution)/shard_map/all_gather | solution.py:38
  7.9 491.7 %all-gather.5.cloned.1.call-start = ((), (), s32[]{:S(2)}) async-start(), calls=%async_computation.3 | async-start | bytes 5898240 | tf_op jit(solution)/shard_map/all_gather | solution.py:47
  518.7 5.5 copy-start.1
  518.7 12.1 %copy-start.2 = (s32[128,8]{0,1:T(8,128)S(1)}, s32[128,8]{0,1:T(8,128)}, u32[]{:S(2)}) copy-start(s32[128,8]{0,1:T(8,128)} %param.7) | copy-start | bytes 12292
  518.7 94.6 %all-to-all-start.1 = ((bf16[4,4,72,1792]{3,2,1,0:T(8,128)(2,1)}), bf16[4,4,72,1792]{3,2,1,0:T(8,128)(2,1)}, u32[]{:S(2)}, u32[]{:S(2)}) async-start(bf16[4,4,72,1792]{3,2,1,0:T(8,128)(2,1)} %copy.38), calls=%async_computation.1 | async-start | bytes 8257536 | tf_op jit(solution)/shard_map/all_to_all | solution.py:51
Sparse Core Ops, SparseCore 0:
  9.6 22.2 all-gather.2
  462.7 36.8 all-gather.4
where the time goes:
time: 640 us; the launch traced here: 635 us
  blocking collectives  374 us (58%)
  waiting for transfers between devices  132 us (21%)
  matrix products  68.1 us (11%)
  local copies, waits for them, and re-layouts  34.7 us (5%)
  between operations  14.2 us (2%)
    all_to_all x1, blocking collectives, body(): lax.all_to_all(buffer, 'expert', split_axis=0, concat_axis=0, tiled=True)  368 us
    all_to_all x1, waiting for transfers between devices, body(): lax.all_to_all(answer.astype(jnp.bfloat16), 'expert', split_axis=0, conca...  81.8 us
    all_gather x1, waiting for transfers between devices, body(): lax.all_gather(hidden, ('helper', 'sub'), axis=3, tiled=True)  37 us
    dot_general x1, matrix products, body(): jnp.einsum('nlcd,ldf->nlcf', received, gate_weight, preferred_element_typ...  28 us
    dot_general x1, matrix products, body(): jnp.einsum('nlcd,ldf->nlcf', received, up_weight, preferred_element_type=...  20 us
    dot_general x1, matrix products, body(): jnp.einsum('nlcf,lfd->nlcd', lax.all_gather(hidden, ('helper', 'sub'), ax...  16.8 us
    gather x1, local copies, waits for them, and re-layouts, body(): padded[sources].reshape(homes, local_experts, capacity, features.shape[1])  13.5 us
  transfers between devices with their start and end apart: 3, of which 3 were waited for; matrix products, arithmetic and copies ran while one was open for 2% of the time, Pallas kernels for 0%

commit v1 on v0

v1 whole, which is shorter than its diff:
```python
import functools

import jax
import jax.numpy as jnp
from jax import lax
from jax.experimental import pallas as pl
from jax.experimental.pallas import tpu as pltpu
from jax.sharding import PartitionSpec as P

CAP = 72
CHUNKS = 7
AHEAD = 2
SLOTS = 2
MESH = pl.DeviceIdType.MESH
F32 = jnp.float32
BF16 = jnp.bfloat16


def barrier_all(axes):
    sem = pltpu.get_barrier_semaphore()
    total = 0
    for name in axes:
        size = lax.axis_size(name)
        me = lax.axis_index(name)
        for d in range(1, size):
            pl.semaphore_signal(
                sem, inc=1, device_id={name: lax.rem(me + d, size)}, device_id_type=MESH
            )
            total += 1
    pl.semaphore_wait(sem, total)


def dispatch_kernel(
    dims, tok_ref, routes_ref, gate_hbm, up_hbm, hid_ref, rank_ref,
    tokbuf, wbuf, rows, acc, places,
    recv, send_z, send_x, send_s, w_sem, r_send, r_recv,
):
    n, h, s, local, chunks, width, ff, experts = dims
    z, x, c = lax.axis_index("expert"), lax.axis_index("helper"), lax.axis_index("sub")
    other = 1 - c
    q_own = x * s + c
    toks = tok_ref.shape[0]

    def weights(k, slot):
        return (
            pltpu.make_async_copy(gate_hbm.at[:, :, k], wbuf.at[slot, 0], w_sem.at[slot, 0]),
            pltpu.make_async_copy(up_hbm.at[:, :, k], wbuf.at[slot, 1], w_sem.at[slot, 1]),
        )

    def copy(k, q, zz, send, target):
        return pltpu.make_async_remote_copy(
            src_ref=tokbuf.at[k, q, zz], dst_ref=tokbuf.at[k, q, zz],
            send_sem=send, recv_sem=recv.at[k, q, zz],
            device_id=target, device_id_type=MESH,
        )

    def to_z(k, d):
        return copy(k, q_own, z, send_z.at[k, d - 1], {"expert": lax.rem(z + d, n)})

    def to_x(k, zz, d):
        return copy(k, q_own, zz, send_x.at[k, zz, d - 1], {"helper": lax.rem(x + d, h)})

    def to_s(k, xx, zz):
        return copy(k, xx * s + c, zz, send_s.at[k, xx, zz], {"sub": other})

    def rank_copy(d):
        return pltpu.make_async_remote_copy(
            src_ref=rank_ref.at[z], dst_ref=rank_ref.at[z],
            send_sem=r_send.at[d - 1], recv_sem=r_recv.at[z],
            device_id={"expert": lax.rem(z + d, n)}, device_id_type=MESH,
        )

    def own(k):
        for d in range(1, n):
            to_z(k, d).start()
        for d in range(1, h):
            to_x(k, z, d).start()
        to_s(k, x, z).start()

    for k in range(SLOTS):
        for w in weights(k, k):
            w.start()
    for k in range(chunks):
        tokbuf[k, q_own, z] = tok_ref[:, k * width:(k + 1) * width]

    ids = lax.broadcasted_iota(jnp.int32, (toks, experts), 1)
    named = jnp.zeros((toks, experts), F32)
    for k in range(routes_ref.shape[1]):
        named = named + jnp.where(routes_ref[:, k:k + 1] == ids, 1.0, 0.0)
    before = lax.broadcasted_iota(jnp.int32, (toks, toks), 0) < lax.broadcasted_iota(jnp.int32, (toks, toks), 1)
    same = lax.broadcasted_iota(jnp.int32, (toks, toks), 0) == lax.broadcasted_iota(jnp.int32, (toks, toks), 1)
    over = (((0,), (0,)), ((), ()))
    earlier = lax.dot_general(named, jnp.where(before, 1.0, 0.0), over, preferred_element_type=F32)
    chosen = lax.dot_general(named, jnp.where(same, 1.0, 0.0), over, preferred_element_type=F32)
    rank_ref[z] = jnp.where(chosen > 0.5, earlier, -1.0)

    barrier_all(("expert", "helper", "sub"))
    for d in range(1, n):
        rank_copy(d).start()
    for k in range(min(AHEAD, chunks)):
        own(k)

    acc[...] = jnp.zeros_like(acc)
    for d in range(1, n):
        zz = lax.rem(z + n - d, n)
        pltpu.make_async_remote_copy(
            src_ref=rank_ref.at[zz], dst_ref=rank_ref.at[zz], send_sem=r_send.at[0],
            recv_sem=r_recv.at[zz], device_id={"sub": other}, device_id_type=MESH,
        ).wait_recv()
    slot_ids = lax.broadcasted_iota(jnp.int32, (CAP, toks), 0).astype(F32)
    for b in range(n):
        for l in range(local):
            line = rank_ref[b, pl.ds(z * local + l, 1), :]
            places[b, l * CAP:(l + 1) * CAP, :] = jnp.where(slot_ids == line, 1.0, 0.0)

    def compute(k):
        slot = lax.rem(k, SLOTS)
        for q in range(h * s):
            parts = []
            for b in range(n):
                parts.append(
                    jnp.dot(places[b].astype(BF16), tokbuf[k, q, b], preferred_element_type=F32)
                )
            for l in range(local):
                stack = jnp.concatenate([p[l * CAP:(l + 1) * CAP] for p in parts], axis=0)
                rows[l, :, q * width:(q + 1) * width] = stack.astype(BF16)
        for w in weights(k, slot):
            w.wait()

        def one(l, carry):
            for m in range(2):
                acc[m, l] += jnp.dot(
                    rows[l], wbuf[slot, m, l].reshape(h * s * width, ff), preferred_element_type=F32
                )
            return carry

        lax.fori_loop(0, local, one, 0)

        @pl.when(k + SLOTS < chunks)
        def _():
            for w in weights(k + SLOTS, slot):
                w.start()

    def step(t, carry):
        @pl.when(t + AHEAD < chunks)
        def _():
            own(t + AHEAD)

        @pl.when(t < chunks)
        def _():
            for d in range(1, n):
                zz = lax.rem(z + n - d, n)
                copy(t, q_own, zz, send_z.at[t, 0], {"sub": other}).wait_recv()
                for e in range(1, h):
                    to_x(t, zz, e).start()
                to_s(t, x, zz).start()

        @pl.when((t >= 1) & (t <= chunks))
        def _():
            k = t - 1
            for d in range(0, n):
                zz = lax.rem(z + n - d, n)
                for e in range(1, h):
                    xx = lax.rem(x + e, h)
                    copy(k, xx * s + c, zz, send_z.at[k, 0], {"sub": other}).wait_recv()
                    to_s(k, xx, zz).start()

        @pl.when(t >= 2)
        def _():
            k = t - 2
            for zz in range(n):
                for xx in range(h):
                    copy(k, xx * s + other, zz, send_z.at[k, 0], {"sub": other}).wait_recv()
            compute(k)

        return carry

    lax.fori_loop(0, chunks + 2, step, 0)

    def finish(l, carry):
        gate = acc[0, l]
        hid_ref[l] = (gate / (1.0 + jnp.exp(-gate)) * acc[1, l]).astype(BF16)
        return carry

    lax.fori_loop(0, local, finish, 0)

    def drain(k, carry):
        for d in range(1, n):
            to_z(k, d).wait_send()
        for zz in range(n):
            for d in range(1, h):
                to_x(k, zz, d).wait_send()
            for xx in range(h):
                to_s(k, xx, zz).wait_send()
        return carry

    lax.fori_loop(0, chunks, drain, 0)
    for d in range(1, n):
        rank_copy(d).wait_send()


def dispatch(tokens, routes, gate_weight, up_weight, experts):
    n, h, s = (lax.axis_size(a) for a in ("expert", "helper", "sub"))
    local, wide, ff = gate_weight.shape
    toks, own = tokens.shape
    width = own // CHUNKS
    shape = (local, h * s, CHUNKS, width, ff)
    dims = (n, h, s, local, CHUNKS, width, ff, experts)
    dma = pltpu.SemaphoreType.DMA
    vmem = pl.BlockSpec(memory_space=pltpu.VMEM)
    hbm = pl.BlockSpec(memory_space=pl.ANY)
    return pl.pallas_call(
        functools.partial(dispatch_kernel, dims),
        out_shape=(
            jax.ShapeDtypeStruct((local, n * CAP, ff), BF16),
            jax.ShapeDtypeStruct((n, experts, toks), F32),
        ),
        in_specs=[vmem, vmem, hbm, hbm],
        out_specs=(vmem, vmem),
        scratch_shapes=[
            pltpu.VMEM((CHUNKS, h * s, n, toks, width), BF16),
            pltpu.VMEM((SLOTS, 2, local, h * s, width, ff), BF16),
            pltpu.VMEM((local, n * CAP, h * s * width), BF16),
            pltpu.VMEM((2, local, n * CAP, ff), F32),
            pltpu.VMEM((n, local * CAP, toks), F32),
            dma((CHUNKS, h * s, n)),
            dma((CHUNKS, max(n - 1, 1))),
            dma((CHUNKS, n, max(h - 1, 1))),
            dma((CHUNKS, h, n)),
            dma((SLOTS, 2)),
            dma((max(n - 1, 1),)),
            dma((n,)),
        ],
        compiler_params=pltpu.CompilerParams(
            collective_id=0, has_side_effects=True, vmem_limit_bytes=60 * 1024 * 1024
        ),
        cost_estimate=pl.CostEstimate(
            flops=4 * local * n * CAP * wide * ff,
            bytes_accessed=4 * local * wide * ff,
            transcendentals=local * n * CAP * ff,
        ),
        name="dispatch_up",
    )(tokens, routes, gate_weight.reshape(shape), up_weight.reshape(shape))


def body(tokens, routes, router_weight, gate_weight, up_weight, down_weight):
    toks = tokens.shape[0]
    experts = router_weight.shape[1]
    n = lax.axis_size("expert")
    local = gate_weight.shape[0]
    partial_logits = jnp.dot(tokens, router_weight, preferred_element_type=F32)
    logits = lax.psum(partial_logits, ("helper", "sub"))
    zloss = jnp.square(jnp.log(jnp.sum(jnp.exp(logits), axis=1)))
    named = jnp.any(routes[:, :, None] == jnp.arange(experts, dtype=jnp.int32), axis=1)
    affinity = jnp.where(named, jax.nn.sigmoid(logits), 0.0)
    gates = (2.5 * affinity / jnp.sum(affinity, axis=1, keepdims=True)).astype(BF16)
    all_gates = lax.all_gather(gates.T, "expert", axis=0)
    hidden, ranks = dispatch(tokens, routes, gate_weight, up_weight, experts)
    home = lax.axis_index("expert") * local
    my_ranks = lax.dynamic_slice_in_dim(ranks, home, local, 1)
    my_gates = lax.dynamic_slice_in_dim(all_gates, home, local, 1)
    slot_ids = jnp.arange(CAP, dtype=F32)[None, None, :, None]
    table = jnp.where(my_ranks[:, :, None, :] == slot_ids, my_gates[:, :, None, :], 0.0).astype(BF16)
    full = lax.all_gather(hidden, ("helper", "sub"), axis=2, tiled=True)
    answer = jnp.einsum("lrf,lfd->lrd", full, down_weight, preferred_element_type=F32).astype(BF16)
    answer = answer.reshape(local, n, CAP, -1)
    part = jnp.einsum("blct,lbcd->btd", table, answer, preferred_element_type=F32).astype(BF16)
    pieces = lax.all_to_all(part, "expert", split_axis=0, concat_axis=0, tiled=True)
    mixed = jnp.sum(pieces.astype(F32), axis=0)
    return (mixed.astype(BF16), zloss)


def solution(mesh):
    placed = (
        P(("groups", "expert"), ("helper", "sub")),
        P(("groups", "expert"), None),
        P(("helper", "sub"), None),
        P("expert", None, ("helper", "sub")),
        P("expert", None, ("helper", "sub")),
        P("expert", None, ("helper", "sub")),
    )
    return jax.shard_map(
        body,
        mesh=mesh,
        in_specs=placed,
        out_specs=(P(("groups", "expert"), ("helper", "sub")), P(("groups", "expert"))),
        check_vma=False,
    )
```

time: 640 us -> 197 us (0.31)
  the two profiles are of different devices: /device:TPU:8 before, /device:TPU:0 now
where the time goes in v1:
time: 197 us; the launch traced here: 196 us
  Pallas kernels  66.4 us (34%)
  waiting for transfers between devices  60.8 us (31%)
  matrix products  25.1 us (13%)
  blocking collectives  21.3 us (11%)
  between operations  14.1 us (7%)
  starting transfers between devices  4.64 us (2%)
  local copies, waits for them, and re-layouts  2.18 us (1%)
    pallas_call x1, Pallas kernels, dispatch(): pl.pallas_call(functools.partial(dispatch_kernel, dims), out_shape=(jax.S...  66.4 us
    all_to_all x1, waiting for transfers between devices, body(): lax.all_to_all(part, 'expert', split_axis=0, concat_axis=0, tiled=True)  42.5 us
    dot_general x1, matrix products, body(): jnp.einsum('lrf,lfd->lrd', full, down_weight, preferred_element_type=F32)  20.3 us
    all_gather x1, waiting for transfers between devices, body(): full = lax.all_gather(hidden, ('helper', 'sub'), axis=2, tiled=True)  18.3 us
    all_gather x1, blocking collectives, body(): all_gates = lax.all_gather(gates.T, 'expert', axis=0)  15.5 us
    psum x1, blocking collectives, body(): logits = lax.psum(partial_logits, ('helper', 'sub'))  5.8 us
    all_to_all x1, starting transfers between devices, body(): lax.all_to_all(part, 'expert', split_axis=0, concat_axis=0, tiled=True)  4.6 us
    dot_general x1, matrix products, body(): jnp.einsum('blct,lbcd->btd', table, answer, preferred_element_type=F32)  4.59 us
  transfers between devices with their start and end apart: 2, of which 2 were waited for; matrix products, arithmetic and copies ran while one was open for 1% of the time, Pallas kernels for 0%

profile of v1, /device:TPU:0, one launch (start us, length us, event | category | flops | bytes accessed | tf_op | source)
XLA Modules:
  0.0 196.2 jit_solution(5843909158068201590)
XLA Ops:
  7.2 0.0 copy-start
  7.2 0.0 all-gather.3.cloned.1.call-start
  7.2 1.4 copy.11.routes_ref
  8.6 0.0 copy-start.2
  8.6 0.0 copy-start.3
  8.6 66.4 %dispatch_up.1 = (bf16[4,288,512]{2,1,0:T(8,128)(2,1)}, f32[4,16,128]{2,1,0:T(8,128)}) custom-call(bf16[128,1792]{1,0:T(8,128)(2,1)} %tok_ref.1, s32[128,8]{1,0:T(8,128)} %copy.11.routes_ref, bf16[4,4,7,256,512]{4,3,2,1,0:T(8,128)(2,1)} %bitcast.14, bf16[4,4,7,256,512]{4,3,2,1,0:T(8,128)(2,1)} %bitcast.15), custom_call_target="tpu_custom_call" | custom-call | flops 16911433728 | bytes 58720256 | tf_op jit(solution)/shard_map/dispatch_up/pallas_call | solution.py:212
  75.1 0.0 all-gather.3.cloned.1.call-update
  75.1 0.0 copy-done
  75.1 0.0 copy-done.2
  75.1 0.2 fusion.13
  75.3 5.8 %psum.7 = f32[128,16]{0,1:T(8,128)S(1)} all-reduce(f32[128,16]{0,1:T(8,128)S(1)} %fusion.13), channel_id=1, replica_groups=mesh['groups'=2,'expert'=4,'helper'=2,'sub'=2] {'helper','sub'}, use_global_device_ids=true, to_apply=%region_1.0 | all-reduce | flops 2048 | bytes 16384 | tf_op jit(solution)/shard_map/psum | solution.py:252
  81.1 0.0 copy-done.3
  81.2 15.5 %all-gather = bf16[64,128]{1,0:T(8,128)(2,1)S(1)} all-gather(bf16[16,128]{1,0:T(8,128)(2,1)S(1)} %fusion.10), channel_id=2, replica_groups=mesh['groups'=2,'expert'=4,'helper'=2,'sub'=2] {'expert'}, dimensions={0}, use_global_device_ids=true | all-gather | bytes 20480 | tf_op jit(solution)/shard_map/all_gather | solution.py:257
  96.7 0.7 constant_dynamic-slice_fusion.1
  97.4 18.3 %all-gather.3.cloned.1.call-done = bf16[4,288,2048]{2,1,0:T(8,128)(2,1)} async-done(((bf16[4,288,512]{2,1,0:T(8,128)(2,1)}), bf16[4,288,2048]{2,1,0:T(8,128)(2,1)}) %all-gather.3.cloned.1.call-update) | async-done | bytes 4718608 | tf_op jit(solution)/shard_map/all_gather | solution.py:264
  115.7 20.3 %convolution_convert_fusion = bf16[4,288,1792]{2,1,0:T(8,128)(2,1)} fusion(bf16[4,288,2048]{2,1,0:T(8,128)(2,1)} %all-gather.3.cloned.1.call-done, bf16[4,2048,1792]{2,1,0:T(8,128)(2,1)} %param.11), kind=kOutput, calls=%fused_computation.2 | convolution fusion | flops 8457781248 | bytes 38207488 | tf_op jit(solution)/shard_map/lrf,lfd->lrd/dot_general | solution.py:265
  136.0 0.0 copy-start.1
  136.0 4.6 %bitcast_convert_fusion = bf16[4,128,1792]{2,1,0:T(8,128)(2,1)} fusion(bf16[4,4,72,1792]{3,2,1,0:T(8,128)(2,1)} %bitcast.16, f32[4,4,128]{2,1,0:T(4,128)S(1)} %constant_dynamic-slice_fusion.1, bf16[4,4,128]{2,1,0:T(4,128)(2,1)S(1)} %constant_dynamic-slice_fusion), kind=kOutput, calls=%fused_computation.3 | convolution fusion | flops 529694720 | bytes 5976064 | tf_op jit(solution)/shard_map/blct,lbcd->btd/dot_general | solution.py:267
  140.6 4.6 %all-to-all-start = ((bf16[4,128,1792]{2,1,0:T(8,128)(2,1)}), bf16[4,128,1792]{2,1,0:T(8,128)(2,1)S(1)}, u32[]{:S(2)}, u32[]{:S(2)}) async-start(bf16[4,128,1792]{2,1,0:T(8,128)(2,1)} %bitcast_convert_fusion), calls=%async_computation | async-start | bytes 3670016 | tf_op jit(solution)/shard_map/all_to_all | solution.py:268
  145.2 0.5 log_multiply_fusion
  145.8 42.5 %all-to-all-done = bf16[4,128,1792]{2,1,0:T(8,128)(2,1)S(1)} async-done(((bf16[4,128,1792]{2,1,0:T(8,128)(2,1)}), bf16[4,128,1792]{2,1,0:T(8,128)(2,1)S(1)}, u32[]{:S(2)}, u32[]{:S(2)}) %all-to-all-start) | async-done | bytes 1835040 | tf_op jit(solution)/shard_map/all_to_all | solution.py:268
  188.2 1.2 reduce_sum.31
  189.4 0.0 copy-done.1
  (4 shorter events, 0.1 us)
Async XLA Ops:
  7.2 67.9 %copy-start = (bf16[1792,16]{0,1:T(8,128)(2,1)S(1)}, bf16[1792,16]{0,1:T(8,128)(2,1)}, u32[]{:S(2)}) copy-start(bf16[1792,16]{0,1:T(8,128)(2,1)} %param.8) | copy-start | bytes 172036
  7.2 108.5 %all-gather.3.cloned.1.call-start = ((), (), s32[]{:S(2)}) async-start(), calls=%async_computation.1 | async-start | bytes 5898240 | tf_op jit(solution)/shard_map/all_gather | solution.py:264
  8.6 66.5 %copy-start.2 = (bf16[128,1792]{1,0:T(8,128)(2,1)S(1)}, bf16[128,1792]{1,0:T(8,128)(2,1)}, u32[]{:S(2)}) copy-start(bf16[128,1792]{1,0:T(8,128)(2,1)} %tok_ref.1) | copy-start | bytes 1376260
  8.6 72.5 %copy-start.3 = (s32[128,8]{0,1:T(8,128)S(1)}, s32[128,8]{0,1:T(8,128)}, u32[]{:S(2)}) copy-start(s32[128,8]{0,1:T(8,128)} %param.7) | copy-start | bytes 12292
  136.0 53.3 %copy-start.1 = (bf16[1792,16]{0,1:T(8,128)(2,1)S(1)}, bf16[1792,16]{0,1:T(8,128)(2,1)}, u32[]{:S(2)}) copy-start(bf16[1792,16]{0,1:T(8,128)(2,1)} %param.8) | copy-start | bytes 172036
  140.6 47.6 %all-to-all-start = ((bf16[4,128,1792]{2,1,0:T(8,128)(2,1)}), bf16[4,128,1792]{2,1,0:T(8,128)(2,1)S(1)}, u32[]{:S(2)}, u32[]{:S(2)}) async-start(bf16[4,128,1792]{2,1,0:T(8,128)(2,1)} %bitcast_convert_fusion), calls=%async_computation | async-start | bytes 3670016 | tf_op jit(solution)/shard_map/all_to_all | solution.py:268
Sparse Core Ops, SparseCore 0:
  75.2 40.4 all-gather.2

commit v2 on v1

v2 whole, which is shorter than its diff:
```python
import functools

import jax
import jax.numpy as jnp
from jax import lax
from jax.experimental import pallas as pl
from jax.experimental.pallas import tpu as pltpu
from jax.sharding import PartitionSpec as P

CAP = 72
CHUNKS = 7
AHEAD = 2
SLOTS = 2
D_SLOTS = 2
VMEM_LIMIT = 62 * 1024 * 1024
MESH = pl.DeviceIdType.MESH
F32 = jnp.float32
BF16 = jnp.bfloat16


def layer_kernel(
    dims, tok_ref, routes_ref, router_ref, gate_hbm, up_hbm, down_hbm, out_ref, zloss_ref,
    tokbuf, wbuf, dbuf, rows, acc, places, table, ranks, gates, logits, hbuf, part, sendbuf, recvbuf,
    recv, send_z, send_x, send_s, w_sem, d_sem, r_send, r_recv, g_send, g_recv, l_send, l_recv,
    h_recv, h_send_x, h_send_s, p_send, p_recv,
):
    n, h, s, local, chunks, width, ff, experts, d_slots = dims
    z, x, c = lax.axis_index("expert"), lax.axis_index("helper"), lax.axis_index("sub")
    other = 1 - c
    q_own = x * s + c
    toks = tok_ref.shape[0]
    nh = n // 2
    half = nh * CAP
    items = 2 * local

    def weights(k, slot):
        return (
            pltpu.make_async_copy(gate_hbm.at[:, :, k], wbuf.at[slot, 0], w_sem.at[slot, 0]),
            pltpu.make_async_copy(up_hbm.at[:, :, k], wbuf.at[slot, 1], w_sem.at[slot, 1]),
        )

    def down(l, slot):
        return pltpu.make_async_copy(down_hbm.at[l], dbuf.at[slot], d_sem.at[slot])

    def remote(src, dst, send, got, target):
        return pltpu.make_async_remote_copy(
            src_ref=src, dst_ref=dst, send_sem=send, recv_sem=got,
            device_id=target, device_id_type=MESH,
        )

    def copy(k, q, zz, send, target):
        ref = tokbuf.at[k, q, zz]
        return remote(ref, ref, send, recv.at[k, q, zz], target)

    def to_z(k, d):
        return copy(k, q_own, z, send_z.at[k, d - 1], {"expert": lax.rem(z + d, n)})

    def to_x(k, zz, d):
        return copy(k, q_own, zz, send_x.at[k, zz, d - 1], {"helper": lax.rem(x + d, h)})

    def to_s(k, xx, zz):
        return copy(k, xx * s + c, zz, send_s.at[k, xx, zz], {"sub": other})

    def rank_copy(d):
        ref = ranks.at[z]
        return remote(ref, ref, r_send.at[d - 1], r_recv.at[z], {"expert": lax.rem(z + d, n)})

    def gate_copy(d):
        ref = gates.at[z]
        return remote(ref, ref, g_send.at[d - 1], g_recv.at[z], {"expert": lax.rem(z + d, n)})

    def logit_copy(d, e):
        ref = logits.at[q_own]
        target = {"helper": lax.rem(x + d, h), "sub": lax.rem(c + e, s)}
        return remote(ref, ref, l_send.at[d, e], l_recv.at[q_own], target)

    peers = [(d, e) for d in range(h) for e in range(s) if d or e]

    def hid_copy(f, l, q, send, target):
        ref = hbuf.at[f, l, q]
        return remote(ref, ref, send, h_recv.at[f, l, q], target)

    def hid_x(f, l, d):
        return hid_copy(f, l, q_own, h_send_x.at[f, l, d - 1], {"helper": lax.rem(x + d, h)})

    def hid_s(f, l, xx):
        return hid_copy(f, l, xx * s + c, h_send_s.at[f, l, xx], {"sub": other})

    def hid_start(f, l):
        for d in range(1, h):
            hid_x(f, l, d).start()
        hid_s(f, l, x).start()

    def back(p):
        return remote(
            sendbuf.at[p], recvbuf.at[p], p_send.at[p], p_recv.at[p],
            {"expert": lax.rem(z + 1 + p, n)},
        )

    def own(k):
        for d in range(1, n):
            to_z(k, d).start()
        for d in range(1, h):
            to_x(k, z, d).start()
        to_s(k, x, z).start()

    for k in range(SLOTS):
        for w in weights(k, k):
            w.start()
    for l in range(min(local, d_slots)):
        down(l, l).start()
    for k in range(chunks):
        tokbuf[k, q_own, z] = tok_ref[:, k * width:(k + 1) * width]

    ids = lax.broadcasted_iota(jnp.int32, (toks, experts), 1)
    named = jnp.zeros((toks, experts), F32)
    for k in range(routes_ref.shape[1]):
        named = named + jnp.where(routes_ref[:, k:k + 1] == ids, 1.0, 0.0)
    before = lax.broadcasted_iota(jnp.int32, (toks, toks), 0) < lax.broadcasted_iota(jnp.int32, (toks, toks), 1)
    same = lax.broadcasted_iota(jnp.int32, (toks, toks), 0) == lax.broadcasted_iota(jnp.int32, (toks, toks), 1)
    over = (((0,), (0,)), ((), ()))
    earlier = lax.dot_general(named, jnp.where(before, 1.0, 0.0), over, preferred_element_type=F32)
    chosen = lax.dot_general(named, jnp.where(same, 1.0, 0.0), over, preferred_element_type=F32)
    ranks[z] = jnp.where(chosen > 0.5, earlier, -1.0)
    mine = jnp.dot(tok_ref[...], router_ref[...], preferred_element_type=F32)
    mine = jnp.concatenate([mine, jnp.zeros((toks, 128 - experts), F32)], axis=1)
    logits[q_own] = mine.T[:experts]

    sem = pltpu.get_barrier_semaphore()
    for d in range(1, n):
        pl.semaphore_signal(sem, inc=1, device_id={"expert": lax.rem(z + d, n)}, device_id_type=MESH)
    for d, e in peers:
        target = {"helper": lax.rem(x + d, h), "sub": lax.rem(c + e, s)}
        pl.semaphore_signal(sem, inc=1, device_id=target, device_id_type=MESH)
    pl.semaphore_wait(sem, n - 1 + len(peers))

    for d, e in peers:
        logit_copy(d, e).start()
    for d in range(1, n):
        rank_copy(d).start()
    for k in range(min(AHEAD, chunks)):
        own(k)

    acc[...] = jnp.zeros_like(acc)
    part[...] = jnp.zeros_like(part)
    for d, e in peers:
        q = lax.rem(x + d, h) * s + lax.rem(c + e, s)
        remote(logits.at[q], logits.at[q], l_send.at[0, 0], l_recv.at[q], {"sub": other}).wait_recv()
    total = logits[0]
    for q in range(1, h * s):
        total = total + logits[q]
    zloss_ref[...] = jnp.square(jnp.log(jnp.sum(jnp.exp(total), axis=0, keepdims=True)))
    affinity = jnp.where(ranks[z] >= 0.0, 1.0 / (1.0 + jnp.exp(-total)), 0.0)
    gates[z] = (2.5 * affinity / jnp.sum(affinity, axis=0, keepdims=True)).astype(BF16).astype(F32)
    for d in range(1, n):
        gate_copy(d).start()
    for d in range(1, n):
        zz = lax.rem(z + n - d, n)
        remote(ranks.at[zz], ranks.at[zz], r_send.at[0], r_recv.at[zz], {"sub": other}).wait_recv()
    slot_ids = lax.broadcasted_iota(jnp.int32, (CAP, toks), 0).astype(F32)
    for b in range(n):
        for l in range(local):
            line = ranks[b, pl.ds(z * local + l, 1), :]
            places[b, l * CAP:(l + 1) * CAP, :] = jnp.where(slot_ids == line, 1.0, 0.0)

    def compute(k):
        slot = lax.rem(k, SLOTS)
        for q in range(h * s):
            parts = []
            for p in range(n):
                b = lax.rem(z + 1 + p, n)
                parts.append(
                    jnp.dot(places[b].astype(BF16), tokbuf[k, q, b], preferred_element_type=F32)
                )
            for l in range(local):
                stack = jnp.concatenate([p[l * CAP:(l + 1) * CAP] for p in parts], axis=0)
                rows[l, :, q * width:(q + 1) * width] = stack.astype(BF16)
        for w in weights(k, slot):
            w.wait()

        def one(l, carry):
            for m in range(2):
                acc[m, l] += jnp.dot(
                    rows[l], wbuf[slot, m, l].reshape(h * s * width, ff), preferred_element_type=F32
                )

            @pl.when(k == chunks - 1)
            def _():
                for f in range(2):
                    gate = acc[0, l, f * half:(f + 1) * half]
                    up = acc[1, l, f * half:(f + 1) * half]
                    hbuf[f, l, q_own] = (gate / (1.0 + jnp.exp(-gate)) * up).astype(BF16)
                hid_start(0, l)

            return carry

        lax.fori_loop(0, local, one, 0)

        @pl.when(k + SLOTS < chunks)
        def _():
            for w in weights(k + SLOTS, slot):
                w.start()

    def step(t, carry):
        @pl.when(t + AHEAD < chunks)
        def _():
            own(t + AHEAD)

        @pl.when(t < chunks)
        def _():
            for d in range(1, n):
                zz = lax.rem(z + n - d, n)
                copy(t, q_own, zz, send_z.at[t, 0], {"sub": other}).wait_recv()
                for e in range(1, h):
                    to_x(t, zz, e).start()
                to_s(t, x, zz).start()

        @pl.when((t >= 1) & (t <= chunks))
        def _():
            k = t - 1
            for d in range(0, n):
                zz = lax.rem(z + n - d, n)
                for e in range(1, h):
                    xx = lax.rem(x + e, h)
                    copy(k, xx * s + c, zz, send_z.at[k, 0], {"sub": other}).wait_recv()
                    to_s(k, xx, zz).start()

        @pl.when(t >= 2)
        def _():
            k = t - 2
            for zz in range(n):
                for xx in range(h):
                    copy(k, xx * s + other, zz, send_z.at[k, 0], {"sub": other}).wait_recv()
            compute(k)

        return carry

    lax.fori_loop(0, chunks + 2, step, 0)
    for l in range(local):
        hid_start(1, l)

    for d in range(1, n):
        zz = lax.rem(z + n - d, n)
        remote(gates.at[zz], gates.at[zz], g_send.at[0], g_recv.at[zz], {"sub": other}).wait_recv()
    blank = jnp.zeros((CAP, toks), F32)
    padded = -(-half // 128) * 128
    for f in range(2):
        for l in range(local):
            lines = []
            for i in range(nh):
                b = lax.rem(z + 1 + f * nh + i, n)
                at = pl.ds(z * local + l, 1)
                block = jnp.where(slot_ids == ranks[b, at, :], gates[b, at, :], 0.0)
                lines.append(jnp.concatenate([block if j == i else blank for j in range(nh)], axis=1))
            if padded > half:
                lines.append(jnp.zeros((padded - half, nh * toks), F32))
            table[f, l] = jnp.concatenate(lines, axis=0).T[:, :half].astype(BF16)

    def hid_forward(i):
        f, l = i // local, lax.rem(i, local)
        for e in range(1, h):
            xx = lax.rem(x + e, h)
            hid_copy(f, l, xx * s + c, h_send_x.at[f, l, 0], {"sub": other}).wait_recv()
            hid_s(f, l, xx).start()

    hid_forward(jnp.int32(0))

    def item(i, carry):
        f, l = i // local, lax.rem(i, local)

        @pl.when(i + 1 < items)
        def _():
            hid_forward(i + 1)

        for xx in range(h):
            hid_copy(f, l, xx * s + other, h_send_x.at[f, l, 0], {"sub": other}).wait_recv()
        slot = lax.rem(i, d_slots)
        if local > d_slots:
            down(l, slot).wait()
        else:
            @pl.when(i < local)
            def _():
                down(l, slot).wait()

        def column(j, inner):
            cols = pl.ds(pl.multiple_of(j * width, width), width)
            answer = jnp.zeros((half, width), F32)
            for q in range(h * s):
                answer = answer + jnp.dot(
                    hbuf[f, l, q], dbuf[slot, q * ff:(q + 1) * ff, cols], preferred_element_type=F32
                )
            part[f, :, cols] += jnp.dot(table[f, l], answer.astype(BF16), preferred_element_type=F32)
            return inner

        lax.fori_loop(0, chunks, column, 0)
        if local > d_slots:
            @pl.when(i + d_slots < items)
            def _():
                down(lax.rem(i + d_slots, local), slot).start()

        for f_done in range(2):
            @pl.when(i == (f_done + 1) * local - 1)
            def _():
                for p in range(f_done * nh, min((f_done + 1) * nh, n - 1)):
                    at = (p - f_done * nh) * toks
                    sendbuf[p] = part[f_done, at:at + toks].astype(BF16)
                    back(p).start()

        return carry

    lax.fori_loop(0, items, item, 0)

    for p in range(n - 1):
        back(p).wait_recv()
    result = part[1, (nh - 1) * toks:]
    for p in range(n - 1):
        result = result + recvbuf[p].astype(F32)
    out_ref[...] = result.astype(BF16)

    def drain(k, carry):
        for d in range(1, n):
            to_z(k, d).wait_send()
        for zz in range(n):
            for d in range(1, h):
                to_x(k, zz, d).wait_send()
            for xx in range(h):
                to_s(k, xx, zz).wait_send()
        return carry

    lax.fori_loop(0, chunks, drain, 0)

    def drain_hidden(l, carry):
        for f in range(2):
            for d in range(1, h):
                hid_x(f, l, d).wait_send()
            for xx in range(h):
                hid_s(f, l, xx).wait_send()
        return carry

    lax.fori_loop(0, local, drain_hidden, 0)
    for d in range(1, n):
        rank_copy(d).wait_send()
        gate_copy(d).wait_send()
        back(d - 1).wait_send()
    for d, e in peers:
        logit_copy(d, e).wait_send()


def body(tokens, routes, router_weight, gate_weight, up_weight, down_weight):
    n, h, s = (lax.axis_size(a) for a in ("expert", "helper", "sub"))
    experts = router_weight.shape[1]
    local, wide, ff = gate_weight.shape
    toks, own = tokens.shape
    width = own // CHUNKS
    q = h * s
    half = n // 2 * CAP
    shape = (local, q, CHUNKS, width, ff)
    d_slots = min(local, D_SLOTS)
    dims = (n, h, s, local, CHUNKS, width, ff, experts, d_slots)
    dma = pltpu.SemaphoreType.DMA
    vmem = pl.BlockSpec(memory_space=pltpu.VMEM)
    hbm = pl.BlockSpec(memory_space=pl.ANY)
    mixed, zloss = pl.pallas_call(
        functools.partial(layer_kernel, dims),
        out_shape=(
            jax.ShapeDtypeStruct((toks, own), BF16),
            jax.ShapeDtypeStruct((1, toks), F32),
        ),
        in_specs=[vmem, vmem, vmem, hbm, hbm, hbm],
        out_specs=(vmem, vmem),
        scratch_shapes=[
            pltpu.VMEM((CHUNKS, q, n, toks, width), BF16),
            pltpu.VMEM((SLOTS, 2, local, q, width, ff), BF16),
            pltpu.VMEM((d_slots, q * ff, own), BF16),
            pltpu.VMEM((local, n * CAP, q * width), BF16),
            pltpu.VMEM((2, local, n * CAP, ff), F32),
            pltpu.VMEM((n, local * CAP, toks), F32),
            pltpu.VMEM((2, local, n // 2 * toks, half), BF16),
            pltpu.VMEM((n, experts, toks), F32),
            pltpu.VMEM((n, experts, toks), F32),
            pltpu.VMEM((q, experts, toks), F32),
            pltpu.VMEM((2, local, q, half, ff), BF16),
            pltpu.VMEM((2, n // 2 * toks, own), F32),
            pltpu.VMEM((n - 1, toks, own), BF16),
            pltpu.VMEM((n - 1, toks, own), BF16),
            dma((CHUNKS, q, n)),
            dma((CHUNKS, n - 1)),
            dma((CHUNKS, n, h - 1)),
            dma((CHUNKS, h, n)),
            dma((SLOTS, 2)),
            dma((d_slots,)),
            dma((n - 1,)),
            dma((n,)),
            dma((n - 1,)),
            dma((n,)),
            dma((h, s)),
            dma((q,)),
            dma((2, local, q)),
            dma((2, local, h - 1)),
            dma((2, local, h)),
            dma((n - 1,)),
            dma((n - 1,)),
        ],
        compiler_params=pltpu.CompilerParams(
            collective_id=0, has_side_effects=True, vmem_limit_bytes=VMEM_LIMIT
        ),
        cost_estimate=pl.CostEstimate(
            flops=6 * local * n * CAP * wide * ff,
            bytes_accessed=6 * local * wide * ff,
            transcendentals=local * n * CAP * ff,
        ),
        name="expert_layer",
    )(
        tokens, routes, router_weight,
        gate_weight.reshape(shape), up_weight.reshape(shape), down_weight,
    )
    return mixed, zloss.reshape(toks)


def solution(mesh):
    placed = (
        P(("groups", "expert"), ("helper", "sub")),
        P(("groups", "expert"), None),
        P(("helper", "sub"), None),
        P("expert", None, ("helper", "sub")),
        P("expert", None, ("helper", "sub")),
        P("expert", None, ("helper", "sub")),
    )
    return jax.shard_map(
        body,
        mesh=mesh,
        in_specs=placed,
        out_specs=(P(("groups", "expert"), ("helper", "sub")), P(("groups", "expert"))),
        check_vma=False,
    )
```

time: 197 us -> 137 us (0.70)
  the two profiles are of different devices: /device:TPU:0 before, /device:TPU:8 now
where the time goes in v2:
time: 137 us; the launch traced here: 136 us
  Pallas kernels  130 us (95%)
  local copies, waits for them, and re-layouts  6.13 us (4%)
    pallas_call x1, Pallas kernels, body(): pl.pallas_call(functools.partial(layer_kernel, dims), out_shape=(jax.Shap...  130 us
    unnamed x4, local copies, waits for them, and re-layouts  6.13 us

profile of v2, /device:TPU:8, one launch (start us, length us, event | category | flops | bytes accessed | tf_op | source)
XLA Modules:
  0.0 136.4 jit_solution(9168439686633078170)
XLA Ops:
  0.6 1.4 %copy.8.routes_ref = s32[128,8]{1,0:T(8,128)} copy(s32[128,8]{0,1:T(8,128)} %param.7) | data formatting | bytes 8192 | tf_op args[1]
  2.0 1.8 %copy.9.router_ref = bf16[1792,16]{1,0:T(8,128)(2,1)} copy(bf16[1792,16]{0,1:T(8,128)(2,1)} %param.8) | data formatting | bytes 114688 | tf_op args[2]
  3.8 129.6 %expert_layer.1 = (bf16[128,1792]{1,0:T(8,128)(2,1)}, f32[1,128]{1,0:T(1,128)}) custom-call(bf16[128,1792]{1,0:T(8,128)(2,1)} %tok_ref.1, s32[128,8]{1,0:T(8,128)} %copy.8.routes_ref, bf16[1792,16]{1,0:T(8,128)(2,1)} %copy.9.router_ref, bf16[4,4,7,256,512]{4,3,2,1,0:T(8,128)(2,1)} %bitcast.3, bf16[4,4,7,256,512]{4,3,2,1,0:T(8,128)(2,1)} %bitcast.4, ...), custom_call_target="tpu_custom_call" | custom-call | flops 25367150592 | bytes 88080384 | tf_op jit(solution)/shard_map/expert_layer/pallas_call | solution.py:363
  133.4 1.8 %copy.12 = bf16[128,1792]{1,0:T(8,128)(2,1)} copy(bf16[128,1792]{1,0:T(8,128)(2,1)} %get-tuple-element.8) | data formatting | bytes 917504
  135.3 1.1 copy.13

commit v3 on v2

--- a/solution.py
+++ b/solution.py
@@ -215,6 +215,14 @@
                     to_x(t, zz, e).start()
                 to_s(t, x, zz).start()
 
+        @pl.when(t >= 2)
+        def _():
+            k = t - 2
+            for zz in range(n):
+                for xx in range(h):
+                    copy(k, xx * s + other, zz, send_z.at[k, 0], {"sub": other}).wait_recv()
+            compute(k)
+
         @pl.when((t >= 1) & (t <= chunks))
         def _():
             k = t - 1
@@ -224,14 +232,6 @@
                     xx = lax.rem(x + e, h)
                     copy(k, xx * s + c, zz, send_z.at[k, 0], {"sub": other}).wait_recv()
                     to_s(k, xx, zz).start()
-
-        @pl.when(t >= 2)
-        def _():
-            k = t - 2
-            for zz in range(n):
-                for xx in range(h):
-                    copy(k, xx * s + other, zz, send_z.at[k, 0], {"sub": other}).wait_recv()
-            compute(k)
 
         return carry
 
@@ -282,17 +282,12 @@
             def _():
                 down(l, slot).wait()
 
-        def column(j, inner):
-            cols = pl.ds(pl.multiple_of(j * width, width), width)
-            answer = jnp.zeros((half, width), F32)
-            for q in range(h * s):
-                answer = answer + jnp.dot(
-                    hbuf[f, l, q], dbuf[slot, q * ff:(q + 1) * ff, cols], preferred_element_type=F32
-                )
+        full = jnp.concatenate([hbuf[f, l, q] for q in range(h * s)], axis=1)
+        for j in range(chunks):
+            cols = slice(j * width, (j + 1) * width)
+            answer = jnp.dot(full, dbuf[slot, :, cols], preferred_element_type=F32)
             part[f, :, cols] += jnp.dot(table[f, l], answer.astype(BF16), preferred_element_type=F32)
-            return inner
-
-        lax.fori_loop(0, chunks, column, 0)
+
         if local > d_slots:
             @pl.when(i + d_slots < items)
             def _():

time: 137 us -> 135 us (0.985)
  Pallas kernels: 130 us -> 128 us
    pallas_call x1, Pallas kernels: 130 us -> 128 us  [body(): pl.pallas_call(functools.partial(layer_kernel, dims), out_shape=(jax.Shap...]
where the time goes in v3:
time: 135 us; the launch traced here: 134 us
  Pallas kernels  128 us (95%)
  local copies, waits for them, and re-layouts  6.13 us (5%)
    pallas_call x1, Pallas kernels, body(): pl.pallas_call(functools.partial(layer_kernel, dims), out_shape=(jax.Shap...  128 us
    unnamed x4, local copies, waits for them, and re-layouts  6.13 us

profile of v3, /device:TPU:8, one launch (start us, length us, event | category | flops | bytes accessed | tf_op | source)
XLA Modules:
  0.0 134.3 jit_solution(10723748614137753286)
XLA Ops:
  0.6 1.4 %copy.8.routes_ref = s32[128,8]{1,0:T(8,128)} copy(s32[128,8]{0,1:T(8,128)} %param.7) | data formatting | bytes 8192 | tf_op args[1]
  2.0 1.8 %copy.9.router_ref = bf16[1792,16]{1,0:T(8,128)(2,1)} copy(bf16[1792,16]{0,1:T(8,128)(2,1)} %param.8) | data formatting | bytes 114688 | tf_op args[2]
  3.8 127.6 %expert_layer.1 = (bf16[128,1792]{1,0:T(8,128)(2,1)}, f32[1,128]{1,0:T(1,128)}) custom-call(bf16[128,1792]{1,0:T(8,128)(2,1)} %tok_ref.1, s32[128,8]{1,0:T(8,128)} %copy.8.routes_ref, bf16[1792,16]{1,0:T(8,128)(2,1)} %copy.9.router_ref, bf16[4,4,7,256,512]{4,3,2,1,0:T(8,128)(2,1)} %bitcast.3, bf16[4,4,7,256,512]{4,3,2,1,0:T(8,128)(2,1)} %bitcast.4, ...), custom_call_target="tpu_custom_call" | custom-call | flops 25367150592 | bytes 88080384 | tf_op jit(solution)/shard_map/expert_layer/pallas_call | solution.py:358
  131.4 1.8 %copy.12 = bf16[128,1792]{1,0:T(8,128)(2,1)} copy(bf16[128,1792]{1,0:T(8,128)(2,1)} %get-tuple-element.8) | data formatting | bytes 917504
  133.2 1.1 copy.13

commit v4 on v3

--- a/solution.py
+++ b/solution.py
@@ -9,7 +9,7 @@
 
 CAP = 72
 CHUNKS = 7
-AHEAD = 2
+AHEAD = 3
 SLOTS = 2
 D_SLOTS = 2
 VMEM_LIMIT = 62 * 1024 * 1024

time: 135 us -> 137 us (1.015)
  Pallas kernels: 128 us -> 130 us
    pallas_call x1, Pallas kernels: 128 us -> 130 us  [body(): pl.pallas_call(functools.partial(layer_kernel, dims), out_shape=(jax.Shap...]
where the time goes in v4:
time: 137 us
  Pallas kernels  130 us (95%)
  local copies, waits for them, and re-layouts  6.13 us (4%)
    pallas_call x1, Pallas kernels, body(): pl.pallas_call(functools.partial(layer_kernel, dims), out_shape=(jax.Shap...  130 us
    unnamed x4, local copies, waits for them, and re-layouts  6.13 us

profile of v4, /device:TPU:8, one launch (start us, length us, event | category | flops | bytes accessed | tf_op | source)
XLA Modules:
  0.0 136.8 jit_solution(8265101603853643202)
XLA Ops:
  0.6 1.4 %copy.8.routes_ref = s32[128,8]{1,0:T(8,128)} copy(s32[128,8]{0,1:T(8,128)} %param.7) | data formatting | bytes 8192 | tf_op args[1]
  2.0 1.8 %copy.9.router_ref = bf16[1792,16]{1,0:T(8,128)(2,1)} copy(bf16[1792,16]{0,1:T(8,128)(2,1)} %param.8) | data formatting | bytes 114688 | tf_op args[2]
  3.8 130.0 %expert_layer.1 = (bf16[128,1792]{1,0:T(8,128)(2,1)}, f32[1,128]{1,0:T(1,128)}) custom-call(bf16[128,1792]{1,0:T(8,128)(2,1)} %tok_ref.1, s32[128,8]{1,0:T(8,128)} %copy.8.routes_ref, bf16[1792,16]{1,0:T(8,128)(2,1)} %copy.9.router_ref, bf16[4,4,7,256,512]{4,3,2,1,0:T(8,128)(2,1)} %bitcast.3, bf16[4,4,7,256,512]{4,3,2,1,0:T(8,128)(2,1)} %bitcast.4, ...), custom_call_target="tpu_custom_call" | custom-call | flops 25367150592 | bytes 88080384 | tf_op jit(solution)/shard_map/expert_layer/pallas_call | solution.py:358
  133.8 1.8 %copy.12 = bf16[128,1792]{1,0:T(8,128)(2,1)} copy(bf16[128,1792]{1,0:T(8,128)(2,1)} %get-tuple-element.8) | data formatting | bytes 917504
  135.7 1.1 copy.13
